TPU v7x, 256 devices: a whole 4x4x8 slice. The times are simulated.
256 devices in a mesh: fluid: 64 (over x, z, core), metal: 4 (over y).
Axes of the slice: x: 4, y: 4, z: 8, core: 2. Of those that a mesh axis runs over, the one named last changes fastest.
Arguments:
- fluid_x: bfloat16 [16384, 512], P('fluid', 'metal'), may hold values from -32 to 32
- metal_x: bfloat16 [8192, 512], P('fluid', 'metal'), may hold values from -32 to 32
- w_rf: bfloat16 [512, 512], P(None, 'metal'), may hold values from -0.5 to 0.5
- w_vf: bfloat16 [512, 512], P(None, 'metal'), may hold values from -0.25 to 0.25
- w_rm: bfloat16 [512, 512], P(None, 'metal'), may hold values from -0.5 to 0.5
- w_vm: bfloat16 [512, 512], P(None, 'metal'), may hold values from -0.25 to 0.25
- fluid_grad: bfloat16 [16384, 512], P('fluid', 'metal'), may hold values from -6 to 6
- metal_grad: bfloat16 [8192, 512], P('fluid', 'metal'), may hold values from -6 to 6
- pair_list: int32 [2048, 2], P('fluid'), may hold values from 0 to 63, as said below
- pair_count: int32 [64], P('fluid'), may hold values from 2 to 32, as said below
Outputs:
- fluid_out: bfloat16 [16384, 512], P('fluid', 'metal')
- metal_out: bfloat16 [8192, 512], P('fluid', 'metal')
- fluid_dx: bfloat16 [16384, 512], P('fluid', 'metal')
- metal_dx: bfloat16 [8192, 512], P('fluid', 'metal')
- weight_grads: float32 [4, 512, 512], P(None, None, 'metal')
Inputs may be any that keep to these rules, and one draw needn't show every extreme that they name: `pair_list`: column 0 is a local fluid block below 2, column 1 a metal block below 64. The first pair_count[d] entries of fluid index d are distinct pairs; every fluid block of every index and every metal block stands in some live entry; entries past the count hold valid indices and are ignored. `pair_count`: some fluid index has all 32 slots live.
All inputs are finite; a program needn't handle non-finite values.
Results may differ from a plain program's by a relative error of at most 0.0179.
The roundings to bfloat16 on the way count: a program that leaves them out, or rounds other values in their place, can miss the bound.
Values may be sent and summed in bfloat16 or wider, within the bound.
No kernel may reach another device: no remote copies, remote signals or barrier semaphores. Data moves between devices by JAX's collectives and lax.ppermute only.
A program may use at most 128 MiB of HBM per device.

v0:
```python
import math
import jax
import jax.numpy as jnp
from jax import lax
from jax.sharding import PartitionSpec as P

D = 512
H = 8
BLK = 128
LOWEST = -1e30


def project(inputs, weight):
    return jnp.dot(inputs, weight, preferred_element_type=jnp.float32).astype(jnp.bfloat16)


def back_project(grads, weight):
    return lax.dot_general(
        grads, weight, (((1,), (1,)), ((), ())), preferred_element_type=jnp.float32
    )


def outer_rows(inputs, grads):
    return lax.dot_general(
        inputs, grads, (((0,), (0,)), ((), ())), preferred_element_type=jnp.float32
    )


def body(fluid_x, metal_x, w_rf, w_vf, w_rm, w_vm, fluid_grad, metal_grad, pair_list, pair_count):
    head_size = D // H
    local_heads = w_rf.shape[1] // head_size
    feature_cols = w_rf.shape[1]
    fluid_rows = fluid_x.shape[0]
    blocks = fluid_rows // BLK
    metal_blocks = lax.axis_size("fluid")
    metal_rows = metal_blocks * BLK
    slot_total = pair_list.shape[0]
    batch_size = math.gcd(slot_total, 16)
    inv_root = 1.0 / math.sqrt(head_size)
    live_count = pair_count[0]
    loop_turns = slot_total // batch_size
    fluid_full, metal_full = (
        lax.all_gather(fluid_x, "metal", axis=1, tiled=True),
        lax.all_gather(metal_x, "metal", axis=1, tiled=True),
    )
    fluid_keys = project(fluid_full, w_rf)
    fluid_values = project(fluid_full, w_vf)
    metal_keys = project(metal_full, w_rm)
    metal_values = project(metal_full, w_vm)
    keys_all, values_all = (
        lax.all_gather(metal_keys, "fluid", axis=0, tiled=True),
        lax.all_gather(metal_values, "fluid", axis=0, tiled=True),
    )
    fkey_tiles = fluid_keys.reshape(blocks, BLK, local_heads, head_size)
    fval_tiles = fluid_values.reshape(blocks, BLK, local_heads, head_size)
    mkey_tiles = keys_all.reshape(metal_blocks, BLK, local_heads, head_size)
    mval_tiles = values_all.reshape(metal_blocks, BLK, local_heads, head_size)

    def batch_pairs(number):
        entries = lax.dynamic_slice_in_dim(pair_list, number * batch_size, batch_size, 0)
        slot_index = number * batch_size + jnp.arange(batch_size, dtype=jnp.int32)
        frows = entries[:, 0]
        mrows = entries[:, 1]
        scores = (
            jnp.einsum(
                "pahd,pbhd->phab",
                fkey_tiles[frows],
                mkey_tiles[mrows],
                preferred_element_type=jnp.float32,
            )
            * inv_root
        )
        return (frows, mrows, slot_index < live_count, scores)

    def max_pass(number, state):
        row_max, col_max = state
        frows, mrows, active, scores = batch_pairs(number)
        live = active[:, None, None]
        row_max = row_max.at[frows].max(jnp.where(live, jnp.max(scores, axis=3), LOWEST))
        col_max = col_max.at[mrows].max(jnp.where(live, jnp.max(scores, axis=2), LOWEST))
        return (row_max, col_max)

    row_max, col_local = lax.fori_loop(
        0,
        loop_turns,
        max_pass,
        (
            jnp.full((blocks, local_heads, BLK), LOWEST, jnp.float32),
            jnp.full((metal_blocks, local_heads, BLK), LOWEST, jnp.float32),
        ),
    )
    col_max = lax.pmax(col_local, "fluid")

    def sum_pass(number, state):
        row_sum, fluid_num, col_sum, metal_num = state
        frows, mrows, active, scores = batch_pairs(number)
        live = active[:, None, None, None]
        row_exp = jnp.where(live, jnp.exp(scores - row_max[frows][:, :, :, None]), 0.0)
        col_exp = jnp.where(live, jnp.exp(scores - col_max[mrows][:, :, None, :]), 0.0)
        row_sum = row_sum.at[frows].add(jnp.sum(row_exp, axis=3))
        col_sum = col_sum.at[mrows].add(jnp.sum(col_exp, axis=2))
        fluid_num = fluid_num.at[frows].add(
            jnp.einsum(
                "phab,pbhd->pahd",
                row_exp.astype(jnp.bfloat16),
                mval_tiles[mrows],
                preferred_element_type=jnp.float32,
            )
        )
        metal_num = metal_num.at[mrows].add(
            jnp.einsum(
                "phab,pahd->pbhd",
                col_exp.astype(jnp.bfloat16),
                fval_tiles[frows],
                preferred_element_type=jnp.float32,
            )
        )
        return (row_sum, fluid_num, col_sum, metal_num)

    row_sum, fluid_num, col_sum, metal_num = lax.fori_loop(
        0,
        loop_turns,
        sum_pass,
        (
            jnp.zeros((blocks, local_heads, BLK), jnp.float32),
            jnp.zeros((blocks, BLK, local_heads, head_size), jnp.float32),
            jnp.zeros((metal_blocks, local_heads, BLK), jnp.float32),
            jnp.zeros((metal_blocks, BLK, local_heads, head_size), jnp.float32),
        ),
    )
    fluid_out = (
        (fluid_num / row_sum.transpose(0, 2, 1)[:, :, :, None])
        .reshape(fluid_rows, feature_cols)
        .astype(jnp.bfloat16)
    )
    num_rows = metal_num.reshape(metal_rows, feature_cols)
    total_rows = col_sum.transpose(0, 2, 1).reshape(metal_rows, local_heads)
    own_num, own_sum = (
        lax.psum_scatter(num_rows, "fluid", scatter_dimension=0, tiled=True),
        lax.psum_scatter(total_rows, "fluid", scatter_dimension=0, tiled=True),
    )
    metal_out = (
        (own_num.reshape(BLK, local_heads, head_size) / own_sum[:, :, None])
        .reshape(BLK, feature_cols)
        .astype(jnp.bfloat16)
    )
    scaled_grad = (
        (metal_grad.astype(jnp.float32).reshape(BLK, local_heads, head_size) / own_sum[:, :, None])
        .reshape(BLK, feature_cols)
        .astype(jnp.bfloat16)
    )
    scaled_all, output_all = (
        lax.all_gather(scaled_grad, "fluid", axis=0, tiled=True),
        lax.all_gather(metal_out, "fluid", axis=0, tiled=True),
    )
    delta_f = jnp.sum(
        (fluid_grad.astype(jnp.float32) * fluid_out.astype(jnp.float32)).reshape(
            fluid_rows, local_heads, head_size
        ),
        axis=2,
    )
    delta_m = jnp.sum(
        (scaled_all.astype(jnp.float32) * output_all.astype(jnp.float32)).reshape(
            metal_blocks, BLK, local_heads, head_size
        ),
        axis=3,
    )
    grad_tiles = fluid_grad.reshape(blocks, BLK, local_heads, head_size)
    scaled_tiles = scaled_all.reshape(metal_blocks, BLK, local_heads, head_size)
    dfluid_tiles = delta_f.reshape(blocks, BLK, local_heads)

    def grad_pass(number, state):
        grad_rf, grad_vf, grad_rm, grad_vm = state
        frows, mrows, active, scores = batch_pairs(number)
        live = active[:, None, None, None]
        attn = jnp.where(
            live,
            jnp.exp(scores - row_max[frows][:, :, :, None]) / row_sum[frows][:, :, :, None],
            0.0,
        )
        col_exp = jnp.where(live, jnp.exp(scores - col_max[mrows][:, :, None, :]), 0.0)
        fluid_term = jnp.einsum(
            "pahd,pbhd->phab",
            grad_tiles[frows],
            mval_tiles[mrows],
            preferred_element_type=jnp.float32,
        )
        metal_term = jnp.einsum(
            "pahd,pbhd->phab",
            fval_tiles[frows],
            scaled_tiles[mrows],
            preferred_element_type=jnp.float32,
        )
        dscore = attn * (fluid_term - dfluid_tiles[frows].transpose(0, 2, 1)[:, :, :, None])
        dscore = dscore + col_exp * (metal_term - delta_m[mrows].transpose(0, 2, 1)[:, :, None, :])
        dscore_weight = dscore.astype(jnp.bfloat16)
        grad_rf = grad_rf.at[frows].add(
            jnp.einsum(
                "phab,pbhd->pahd",
                dscore_weight,
                mkey_tiles[mrows],
                preferred_element_type=jnp.float32,
            )
            * inv_root
        )
        grad_vf = grad_vf.at[frows].add(
            jnp.einsum(
                "phab,pbhd->pahd",
                col_exp.astype(jnp.bfloat16),
                scaled_tiles[mrows],
                preferred_element_type=jnp.float32,
            )
        )
        grad_rm = grad_rm.at[mrows].add(
            jnp.einsum(
                "phab,pahd->pbhd",
                dscore_weight,
                fkey_tiles[frows],
                preferred_element_type=jnp.float32,
            )
            * inv_root
        )
        grad_vm = grad_vm.at[mrows].add(
            jnp.einsum(
                "phab,pahd->pbhd",
                attn.astype(jnp.bfloat16),
                grad_tiles[frows],
                preferred_element_type=jnp.float32,
            )
        )
        return (grad_rf, grad_vf, grad_rm, grad_vm)

    grad_rf, grad_vf, grad_rm, grad_vm = lax.fori_loop(
        0,
        loop_turns,
        grad_pass,
        (
            jnp.zeros((blocks, BLK, local_heads, head_size), jnp.float32),
            jnp.zeros((blocks, BLK, local_heads, head_size), jnp.float32),
            jnp.zeros((metal_blocks, BLK, local_heads, head_size), jnp.float32),
            jnp.zeros((metal_blocks, BLK, local_heads, head_size), jnp.float32),
        ),
    )
    rf_rounded = grad_rf.reshape(fluid_rows, feature_cols).astype(jnp.bfloat16)
    vf_rounded = grad_vf.reshape(fluid_rows, feature_cols).astype(jnp.bfloat16)
    fluid_part = back_project(rf_rounded, w_rf) + back_project(vf_rounded, w_vf)
    fluid_part, weight_rf, weight_vf = (
        fluid_part,
        outer_rows(fluid_full, rf_rounded),
        outer_rows(fluid_full, vf_rounded),
    )
    rm_rounded = lax.psum_scatter(
        grad_rm.reshape(metal_rows, feature_cols), "fluid", scatter_dimension=0, tiled=True
    ).astype(jnp.bfloat16)
    vm_rounded = lax.psum_scatter(
        grad_vm.reshape(metal_rows, feature_cols), "fluid", scatter_dimension=0, tiled=True
    ).astype(jnp.bfloat16)
    metal_part = back_project(rm_rounded, w_rm) + back_project(vm_rounded, w_vm)
    weight_rm = outer_rows(metal_full, rm_rounded)
    weight_vm = outer_rows(metal_full, vm_rounded)
    fluid_dx, metal_dx = (
        lax.psum_scatter(fluid_part, "metal", scatter_dimension=1, tiled=True),
        lax.psum_scatter(metal_part, "metal", scatter_dimension=1, tiled=True),
    )
    weight_grads = lax.psum(jnp.stack([weight_rf, weight_vf, weight_rm, weight_vm]), "fluid")
    return (
        fluid_out,
        metal_out,
        fluid_dx.astype(jnp.bfloat16),
        metal_dx.astype(jnp.bfloat16),
        weight_grads,
    )


def solution(mesh):
    placed = (
        P("fluid", "metal"),
        P("fluid", "metal"),
        P(None, "metal"),
        P(None, "metal"),
        P(None, "metal"),
        P(None, "metal"),
        P("fluid", "metal"),
        P("fluid", "metal"),
        P("fluid", None),
        P("fluid"),
    )
    return jax.shard_map(
        body,
        mesh=mesh,
        in_specs=placed,
        out_specs=(
            P("fluid", "metal"),
            P("fluid", "metal"),
            P("fluid", "metal"),
            P("fluid", "metal"),
            P(None, None, "metal"),
        ),
        check_vma=False,
    )
```

profile of v0, /device:TPU:2, one launch (start us, length us, event | category | flops | bytes accessed | tf_op | source)
XLA Modules:
  0.0 1555.2 jit_solution(13822160661187020611)
XLA Ops:
  7.2 11.8 all_gather.19
  22.6 11.7 all_gather.18
  34.7 64.7 %all-gather.5.cloned.1.call-done = bf16[8192,128]{1,0:T(8,128)(2,1)} async-done(((bf16[128,128]{1,0:T(8,128)(2,1)}), bf16[8192,128]{1,0:T(8,128)(2,1)}) %all-gather.5.cloned.1.call-update) | async-done | bytes 2097168 | tf_op jit(solution)/shard_map/all_gather | solution.py:51
  99.4 8.2 reshape.334
  107.6 23.2 %while.53 = (s32[]{:T(128)}, f32[2,2,128]{2,1,0:T(2,128)S(1)}, f32[64,2,128]{2,1,0:T(2,128)S(1)}, s32[32,2]{0,1:T(2,128)S(1)}, s32[]{:T(128)}, /*index=5*/bf16[2...) while((s32[]{:T(128)}, f32[2,2,128]{2,1,0:T(2,128)S(1)}, ...), condition=%wide.region_5.6_spmd, body=%wide.region_0.5_spmd.sunk | while | flops 68692104 | bytes 3351623 | solution.py:83
  131.9 45.8 %all-gather.7.cloned.1.call-done = bf16[8192,128]{1,0:T(8,128)(2,1)} async-done(((bf16[128,128]{1,0:T(8,128)(2,1)}), bf16[8192,128]{1,0:T(8,128)(2,1)}) %all-gather.7.cloned.1.call-update) | async-done | bytes 2097168 | tf_op jit(solution)/shard_map/all_gather | solution.py:52
  177.7 8.3 reshape.335
  185.9 161.9 %all-reduce.3.cloned.1.call-done = f32[64,2,128]{2,1,0:T(2,128)} async-done(((f32[64,2,128]{2,1,0:T(2,128)}), f32[64,2,128]{2,1,0:T(2,128)}) %all-reduce.3.cloned.1.call-update) | async-done | bytes 65552 | tf_op jit(solution)/shard_map/pmax | solution.py:92
  350.3 67.5 %while.54 = (s32[]{:T(128)}, f32[2,2,128]{2,1,0:T(2,128)S(1)}, f32[2,128,2,64]{1,3,2,0:T(8,128)S(1)}, f32[64,2,128]{2,1,0:T(2,128)S(1)}, f32[64,128,2,64]{1,3,2,...) while((s32[]{:T(128)}, f32[2,2,128]{2,1,0:T(2,128)S(1)}, ...), condition=%wide.region_14.15_spmd, body=%wide.region_7.14_spmd.sunk | while | flops 209717376 | bytes 25437748 | solution.py:120
  358.2 5.7 gather_fusion.4
  391.6 5.7 gather_fusion.4
  431.3 130.0 %reduce-scatter.19.cloned.1.call-done = f32[128,2]{1,0:T(8,128)} async-done(((f32[8192,2]{1,0:T(8,128)}), f32[128,2]{1,0:T(8,128)}) %reduce-scatter.19.cloned.1.call-update) | async-done | bytes 1040
  562.2 145.2 %reduce-scatter.9.cloned.1.call-done = f32[128,128]{0,1:T(8,128)} async-done(((f32[8192,128]{0,1:T(8,128)}), f32[128,128]{0,1:T(8,128)}) %reduce-scatter.9.cloned.1.call-update) | async-done | bytes 65552 | tf_op jit(solution)/shard_map/reduce_scatter | solution.py:139
  710.1 72.3 %all-gather.9.cloned.1.call-done = bf16[8192,128]{0,1:T(8,128)(2,1)} async-done(((bf16[128,128]{0,1:T(8,128)(2,1)}), bf16[8192,128]{0,1:T(8,128)(2,1)}) %all-gather.9.cloned.1.call-update) | async-done | bytes 2097168 | tf_op jit(solution)/shard_map/all_gather | solution.py:153
  782.4 74.9 %all-gather.11.cloned.1.call-done = bf16[8192,128]{0,1:T(8,128)(2,1)} async-done(((bf16[128,128]{0,1:T(8,128)(2,1)}), bf16[8192,128]{0,1:T(8,128)(2,1)}) %all-gather.11.cloned.1.call-update) | async-done | bytes 2097168 | tf_op jit(solution)/shard_map/all_gather | solution.py:154
  877.5 131.7 %while.55 = (s32[]{:T(128)}, f32[2,128,2,64]{1,3,2,0:T(8,128)S(1)}, f32[2,128,2,64]{1,3,2,0:T(8,128)S(1)}, f32[64,128,2,64]{1,3,2,0:T(8,128)}, f32[64,128,2,64]{...) while((s32[]{:T(128)}, f32[2,128,2,64]{1,3,2,0:T(8,128)S(1)}, ...), condition=%wide.region_24.25_spmd, body=%wide.region_19.24_spmd.sunk | while | flops 482347136 | bytes 61189336 | solution.py:233
  895.4 5.7 gather_fusion.8
  961.1 5.7 gather_fusion.8
  1023.8 5.3 copy.185
  1031.5 129.8 %reduce-scatter.15.cloned.1.call-done = f32[128,128]{0,1:T(8,128)} async-done(((f32[8192,128]{0,1:T(8,128)}), f32[128,128]{0,1:T(8,128)}) %reduce-scatter.15.cloned.1.call-update) | async-done | bytes 65552 | tf_op jit(solution)/shard_map/reduce_scatter | solution.py:255
  1162.3 145.3 %reduce-scatter.13.cloned.1.call-done = f32[128,128]{0,1:T(8,128)} async-done(((f32[8192,128]{0,1:T(8,128)}), f32[128,128]{0,1:T(8,128)}) %reduce-scatter.13.cloned.1.call-update) | async-done | bytes 65552 | tf_op jit(solution)/shard_map/reduce_scatter | solution.py:252
  1312.6 20.7 %reduce-scatter.11.cloned.1.call-done = f32[256,128]{1,0:T(8,128)} async-done(((f32[256,512]{1,0:T(8,128)}), f32[256,128]{1,0:T(8,128)}) %reduce-scatter.11.cloned.1.call-update) | async-done | bytes 131088 | tf_op jit(solution)/shard_map/reduce_scatter | solution.py:262
  1334.8 188.6 %all-reduce.5.cloned.1.call-done = f32[4,512,128]{1,2,0:T(8,128)} async-done(((f32[4,512,128]{1,2,0:T(8,128)}), f32[4,512,128]{1,2,0:T(8,128)}) %all-reduce.5.cloned.1.call-update) | async-done | bytes 1048592 | tf_op jit(solution)/shard_map/psum | solution.py:265
  1525.9 20.6 %reduce-scatter.17.cloned.1.call-done = f32[128,128]{1,0:T(8,128)} async-done(((f32[128,512]{1,0:T(8,128)}), f32[128,128]{1,0:T(8,128)}) %reduce-scatter.17.cloned.1.call-update) | async-done | bytes 65552 | tf_op jit(solution)/shard_map/reduce_scatter | solution.py:263
  (269 shorter events, 270.7 us)
Async XLA Ops:
  7.2 27.2 %copy-start = (bf16[512,128]{1,0:T(8,128)(2,1)S(1)}, bf16[512,128]{1,0:T(8,128)(2,1)}, u32[]{:S(2)}) copy-start(bf16[512,128]{1,0:T(8,128)(2,1)} %param.18) | copy-start | bytes 393220
  7.2 92.2 %all-gather.5.cloned.1.call-start = ((), (), s32[]{:S(2)}) async-start(), calls=%async_computation.6 | async-start | bytes 2129920 | tf_op jit(solution)/shard_map/all_gather | solution.py:51
  19.0 15.3 copy-start.8
  20.8 156.9 %all-gather.7.cloned.1.call-start = ((), (), s32[]{:S(2)}) async-start(), calls=%async_computation.7 | async-start | bytes 2129920 | tf_op jit(solution)/shard_map/all_gather | solution.py:52
  22.6 325.3 %all-reduce.3.cloned.1.call-start = ((), (), s32[]{:S(2)}) async-start(), calls=%async_computation.8 | async-start | bytes 131072 | tf_op jit(solution)/shard_map/pmax | solution.py:92
  34.3 97.2 %copy-start.6 = (bf16[256,512]{1,0:T(8,128)(2,1)}, bf16[256,512]{1,0:T(8,128)(2,1)S(1)}, u32[]{:S(2)}) copy-start(bf16[256,512]{1,0:T(8,128)(2,1)S(1)} %all_gather.18) | copy-start | bytes 786436
  34.7 72.9 %copy-start.22 = (s32[32,2]{0,1:T(2,128)S(1)}, s32[32,2]{0,1:T(2,128)}, u32[]{:S(2)}) copy-start(s32[32,2]{0,1:T(2,128)} %param.24) | copy-start | bytes 772
  107.6 24.0 %copy-start.13 = (bf16[512,128]{1,0:T(8,128)(2,1)S(1)}, bf16[512,128]{1,0:T(8,128)(2,1)}, u32[]{:S(2)}) copy-start(bf16[512,128]{1,0:T(8,128)(2,1)} %param.19) | copy-start | bytes 393220
  131.5 429.8 %reduce-scatter.19.cloned.1.call-start = ((), (), s32[]{:S(2)}) async-start(), calls=%async_computation.17 | async-start | bytes 4259840
  410.1 3.9 copy-start.1
  420.5 286.9 %reduce-scatter.9.cloned.1.call-start = ((), (), s32[]{:S(2)}) async-start(), calls=%async_computation.9 | async-start | bytes 4259840 | tf_op jit(solution)/shard_map/reduce_scatter | solution.py:139
  430.4 279.3 %copy-start.20 = (bf16[256,128]{1,0:T(8,128)(2,1)S(1)}, bf16[256,128]{1,0:T(8,128)(2,1)}, u32[]{:S(2)}) copy-start(bf16[256,128]{1,0:T(8,128)(2,1)} %param.22) | copy-start | bytes 196612
  430.5 351.9 %all-gather.9.cloned.1.call-start = ((), (), s32[]{:S(2)}) async-start(), calls=%async_computation.10 | async-start | bytes 2129920 | tf_op jit(solution)/shard_map/all_gather | solution.py:153
  708.9 148.3 %all-gather.11.cloned.1.call-start = ((), (), s32[]{:S(2)}) async-start(), calls=%async_computation.11 | async-start | bytes 2129920 | tf_op jit(solution)/shard_map/all_gather | solution.py:154
  709.7 451.6 %reduce-scatter.15.cloned.1.call-start = ((), (), s32[]{:S(2)}) async-start(), calls=%async_computation.14 | async-start | bytes 4259840 | tf_op jit(solution)/shard_map/reduce_scatter | solution.py:255
  710.0 149.9 %copy-start.11 = (bf16[2,128,2,64]{1,0,3,2:T(2,128)(2,1)}, bf16[2,128,2,64]{1,0,3,2:T(2,128)(2,1)S(1)}, u32[]{:S(2)}) copy-start(bf16[2,128,2,64]{1,0,3,2:T(2,128)(2,1)S(1)} %copy.104) | copy-start | bytes 196612
  1019.1 288.5 %reduce-scatter.13.cloned.1.call-start = ((), (), s32[]{:S(2)}) async-start(), calls=%async_computation.13 | async-start | bytes 4259840 | tf_op jit(solution)/shard_map/reduce_scatter | solution.py:252
  1029.1 304.2 %reduce-scatter.11.cloned.1.call-start = ((), (), s32[]{:S(2)}) async-start(), calls=%async_computation.12 | async-start | bytes 655360 | tf_op jit(solution)/shard_map/reduce_scatter | solution.py:262
  1029.1 132.1 %copy-start.9 = (bf16[128,512]{1,0:T(8,128)(2,1)S(1)}, bf16[128,512]{1,0:T(8,128)(2,1)}, u32[]{:S(2)}) copy-start(bf16[128,512]{1,0:T(8,128)(2,1)} %copy-done.8) | copy-start | bytes 393220
  1031.0 492.3 %all-reduce.5.cloned.1.call-start = ((), (), s32[]{:S(2)}) async-start(), calls=%async_computation.16 | async-start | bytes 2097152 | tf_op jit(solution)/shard_map/psum | solution.py:265
  1031.5 278.4 %copy-start.15 = (bf16[512,128]{1,0:T(8,128)(2,1)S(1)}, bf16[512,128]{1,0:T(8,128)(2,1)}, u32[]{:S(2)}) copy-start(bf16[512,128]{1,0:T(8,128)(2,1)} %param.20) | copy-start | bytes 393220
  1162.3 147.8 %copy-start.16 = (bf16[512,128]{1,0:T(8,128)(2,1)S(1)}, bf16[512,128]{1,0:T(8,128)(2,1)}, u32[]{:S(2)}) copy-start(bf16[512,128]{1,0:T(8,128)(2,1)} %param.21) | copy-start | bytes 393220
  1162.3 147.8 %copy-start.21 = (f32[128,128]{0,1:T(8,128)S(1)}, f32[128,128]{0,1:T(8,128)}, u32[]{:S(2)}) copy-start(f32[128,128]{0,1:T(8,128)} %reduce-scatter.15.cloned.1.call-done) | copy-start | bytes 196612
  1309.8 236.7 %reduce-scatter.17.cloned.1.call-start = ((), (), s32[]{:S(2)}) async-start(), calls=%async_computation.15 | async-start | bytes 327680 | tf_op jit(solution)/shard_map/reduce_scatter | solution.py:263
  (28 other events, 49.7 us)
Sparse Core Ops, SparseCore 0:
  20.9 78.4 all-gather.4
  102.7 74.9 all-gather.6
  181.8 166.0 all-reduce.2
  420.7 140.5 reduce-scatter.18
  565.3 142.0 reduce-scatter.8
  710.7 71.6 all-gather.8
  785.8 71.3 all-gather.10
  1019.2 141.9 reduce-scatter.14
  1165.4 142.1 reduce-scatter.12
  1310.2 23.0 reduce-scatter.10
  1337.7 185.6 all-reduce.4
  1525.7 20.7 reduce-scatter.16
where the time goes:
time: 1570 us; the launch traced here: 1560 us
  waiting for transfers between devices  1200 us (76%)
  local copies, waits for them, and re-layouts  209 us (13%)
  other arithmetic  58.9 us (4%)
  matrix products  46.7 us (3%)
  blocking collectives  23.5 us (1%)
    psum x1, waiting for transfers between devices, body(): lax.psum(jnp.stack([weight_rf, weight_vf, weight_rm, weight_vm]), 'fluid')  189 us
    pmax x1, waiting for transfers between devices, body(): col_max = lax.pmax(col_local, 'fluid')  162 us
    reduce_scatter x1, waiting for transfers between devices, body(): lax.psum_scatter(grad_rm.reshape(metal_rows, feature_cols), 'fluid', scat...  145 us
    reduce_scatter x1, waiting for transfers between devices, body(): lax.psum_scatter(num_rows, 'fluid', scatter_dimension=0, tiled=True)  145 us
    unnamed x13, waiting for transfers between devices  131 us
    reduce_scatter x1, waiting for transfers between devices, body(): lax.psum_scatter(grad_vm.reshape(metal_rows, feature_cols), 'fluid', scat...  130 us
    all_gather x1, waiting for transfers between devices, body(): lax.all_gather(metal_out, 'fluid', axis=0, tiled=True)  74.9 us
    all_gather x1, waiting for transfers between devices, body(): lax.all_gather(scaled_grad, 'fluid', axis=0, tiled=True)  72.3 us
  transfers between devices with their start and end apart: 12, of which 12 were waited for; matrix products, arithmetic and copies ran while one was open for 5% of the time, Pallas kernels for 0%

commit v1 on v0

--- a/solution.py
+++ b/solution.py
@@ -8,6 +8,11 @@
 H = 8
 BLK = 128
 LOWEST = -1e30
+
+
+def gather_from_all(array, axis, dim):
+    copies = jnp.concatenate([array] * lax.axis_size(axis), axis=dim)
+    return lax.all_to_all(copies, axis, dim, dim, tiled=True)
 
 
 def project(inputs, weight):
@@ -150,7 +155,7 @@
         .astype(jnp.bfloat16)
     )
     scaled_all, output_all = (
-        lax.all_gather(scaled_grad, "fluid", axis=0, tiled=True),
+        gather_from_all(scaled_grad, "fluid", 0),
         lax.all_gather(metal_out, "fluid", axis=0, tiled=True),
     )
     delta_f = jnp.sum(

time: 1570 us -> 1510 us (0.962)
  waiting for transfers between devices: 1200 us -> 1120 us
    all_gather x1 -> x0, waiting for transfers between devices: 72.3 us -> none  [body(): lax.all_gather(scaled_grad, 'fluid', axis=0, tiled=True)]
    unnamed x13 -> x12, waiting for transfers between devices: 131 us -> 130 us
  transfers between devices with their start and end apart: 12 -> 12, of which waited for: 12 -> 11; matrix products, arithmetic and copies ran while one was open for 5% -> 5% of each run, Pallas kernels for 0% -> 0%
where the time goes in v1:
time: 1510 us; the launch traced here: 1500 us
  waiting for transfers between devices  1120 us (74%)
  local copies, waits for them, and re-layouts  211 us (14%)
  other arithmetic  58.3 us (4%)
  matrix products  46.7 us (3%)
  blocking collectives  23.5 us (2%)
    psum x1, waiting for transfers between devices, body(): lax.psum(jnp.stack([weight_rf, weight_vf, weight_rm, weight_vm]), 'fluid')  188 us
    pmax x1, waiting for transfers between devices, body(): col_max = lax.pmax(col_local, 'fluid')  162 us
    reduce_scatter x1, waiting for transfers between devices, body(): lax.psum_scatter(num_rows, 'fluid', scatter_dimension=0, tiled=True)  145 us
    reduce_scatter x1, waiting for transfers between devices, body(): lax.psum_scatter(grad_rm.reshape(metal_rows, feature_cols), 'fluid', scat...  145 us
    unnamed x12, waiting for transfers between devices  130 us
    reduce_scatter x1, waiting for transfers between devices, body(): lax.psum_scatter(grad_vm.reshape(metal_rows, feature_cols), 'fluid', scat...  130 us
    all_gather x1, waiting for transfers between devices, body(): lax.all_gather(metal_out, 'fluid', axis=0, tiled=True)  70 us
    all_gather x1, waiting for transfers between devices, body(): lax.all_gather(metal_keys, 'fluid', axis=0, tiled=True)  64.7 us
  transfers between devices with their start and end apart: 12, of which 11 were waited for; matrix products, arithmetic and copies ran while one was open for 5% of the time, Pallas kernels for 0%

profile of v1, /device:TPU:2, one launch (start us, length us, event | category | flops | bytes accessed | tf_op | source)
XLA Modules:
  0.0 1497.3 jit_solution(8792986429646984261)
XLA Ops:
  7.2 11.8 all_gather.16
  22.6 11.7 all_gather.15
  34.7 64.7 %all-gather.4.cloned.1.call-done = bf16[8192,128]{1,0:T(8,128)(2,1)} async-done(((bf16[128,128]{1,0:T(8,128)(2,1)}), bf16[8192,128]{1,0:T(8,128)(2,1)}) %all-gather.4.cloned.1.call-update) | async-done | bytes 2097168 | tf_op jit(solution)/shard_map/all_gather | solution.py:56
  99.4 8.2 reshape.340
  107.6 23.2 %while.53 = (s32[]{:T(128)}, f32[2,2,128]{2,1,0:T(2,128)S(1)}, f32[64,2,128]{2,1,0:T(2,128)S(1)}, s32[32,2]{0,1:T(2,128)S(1)}, s32[]{:T(128)}, /*index=5*/bf16[2...) while((s32[]{:T(128)}, f32[2,2,128]{2,1,0:T(2,128)S(1)}, ...), condition=%wide.region_5.6_spmd, body=%wide.region_0.5_spmd.sunk | while | flops 68692104 | bytes 3351623 | solution.py:88
  131.9 45.8 %all-gather.6.cloned.1.call-done = bf16[8192,128]{1,0:T(8,128)(2,1)} async-done(((bf16[128,128]{1,0:T(8,128)(2,1)}), bf16[8192,128]{1,0:T(8,128)(2,1)}) %all-gather.6.cloned.1.call-update) | async-done | bytes 2097168 | tf_op jit(solution)/shard_map/all_gather | solution.py:57
  177.7 8.3 reshape.341
  186.0 161.9 %all-reduce.3.cloned.1.call-done = f32[64,2,128]{2,1,0:T(2,128)} async-done(((f32[64,2,128]{2,1,0:T(2,128)}), f32[64,2,128]{2,1,0:T(2,128)}) %all-reduce.3.cloned.1.call-update) | async-done | bytes 65552 | tf_op jit(solution)/shard_map/pmax | solution.py:97
  350.3 77.0 %while.54 = (s32[]{:T(128)}, f32[2,2,128]{2,1,0:T(2,128)S(1)}, f32[2,128,2,64]{1,3,2,0:T(8,128)S(1)}, f32[64,2,128]{2,1,0:T(2,128)S(1)}, f32[64,128,2,64]{1,3,2,...) while((s32[]{:T(128)}, f32[2,2,128]{2,1,0:T(2,128)S(1)}, ...), condition=%wide.region_14.15_spmd, body=%wide.region_7.14_spmd.sunk | while | flops 209717376 | bytes 25437748 | solution.py:125
  367.8 5.7 gather_fusion.4
  401.2 5.7 gather_fusion.4
  440.8 130.1 %reduce-scatter.19.cloned.1.call-done = f32[128,2]{1,0:T(8,128)} async-done(((f32[8192,2]{1,0:T(8,128)}), f32[128,2]{1,0:T(8,128)}) %reduce-scatter.19.cloned.1.call-update) | async-done | bytes 1040
  571.8 145.2 %reduce-scatter.9.cloned.1.call-done = f32[128,128]{0,1:T(8,128)} async-done(((f32[8192,128]{0,1:T(8,128)}), f32[128,128]{0,1:T(8,128)}) %reduce-scatter.9.cloned.1.call-update) | async-done | bytes 65552 | tf_op jit(solution)/shard_map/reduce_scatter | solution.py:144
  721.7 8.5 all-to-all-start
  730.6 70.0 %all-gather.8.cloned.1.call-done = bf16[8192,128]{0,1:T(8,128)(2,1)} async-done(((bf16[128,128]{0,1:T(8,128)(2,1)}), bf16[8192,128]{0,1:T(8,128)(2,1)}) %all-gather.8.cloned.1.call-update) | async-done | bytes 2097168 | tf_op jit(solution)/shard_map/all_gather | solution.py:159
  807.9 7.5 copy.118
  820.4 131.7 %while.55 = (s32[]{:T(128)}, f32[2,128,2,64]{1,3,2,0:T(8,128)S(1)}, f32[2,128,2,64]{1,3,2,0:T(8,128)S(1)}, f32[64,128,2,64]{1,3,2,0:T(8,128)}, f32[64,128,2,64]{...) while((s32[]{:T(128)}, f32[2,128,2,64]{1,3,2,0:T(8,128)S(1)}, ...), condition=%wide.region_24.25_spmd, body=%wide.region_19.24_spmd.sunk | while | flops 482347136 | bytes 61189336 | solution.py:238
  838.2 5.7 gather_fusion.8
  903.9 5.7 gather_fusion.8
  974.3 130.1 %reduce-scatter.15.cloned.1.call-done = f32[128,128]{0,1:T(8,128)} async-done(((f32[8192,128]{0,1:T(8,128)}), f32[128,128]{0,1:T(8,128)}) %reduce-scatter.15.cloned.1.call-update) | async-done | bytes 65552 | tf_op jit(solution)/shard_map/reduce_scatter | solution.py:260
  1105.4 145.2 %reduce-scatter.13.cloned.1.call-done = f32[128,128]{0,1:T(8,128)} async-done(((f32[8192,128]{0,1:T(8,128)}), f32[128,128]{0,1:T(8,128)}) %reduce-scatter.13.cloned.1.call-update) | async-done | bytes 65552 | tf_op jit(solution)/shard_map/reduce_scatter | solution.py:257
  1255.6 20.8 %reduce-scatter.11.cloned.1.call-done = f32[256,128]{1,0:T(8,128)} async-done(((f32[256,512]{1,0:T(8,128)}), f32[256,128]{1,0:T(8,128)}) %reduce-scatter.11.cloned.1.call-update) | async-done | bytes 131088 | tf_op jit(solution)/shard_map/reduce_scatter | solution.py:267
  1277.9 187.7 %all-reduce.5.cloned.1.call-done = f32[4,512,128]{1,2,0:T(8,128)} async-done(((f32[4,512,128]{1,2,0:T(8,128)}), f32[4,512,128]{1,2,0:T(8,128)}) %all-reduce.5.cloned.1.call-update) | async-done | bytes 1048592 | tf_op jit(solution)/shard_map/psum | solution.py:270
  1468.2 20.8 %reduce-scatter.17.cloned.1.call-done = f32[128,128]{1,0:T(8,128)} async-done(((f32[128,512]{1,0:T(8,128)}), f32[128,128]{1,0:T(8,128)}) %reduce-scatter.17.cloned.1.call-update) | async-done | bytes 65552 | tf_op jit(solution)/shard_map/reduce_scatter | solution.py:268
  (332 shorter events, 270.0 us)
Async XLA Ops:
  7.2 27.2 %copy-start = (bf16[512,128]{1,0:T(8,128)(2,1)S(1)}, bf16[512,128]{1,0:T(8,128)(2,1)}, u32[]{:S(2)}) copy-start(bf16[512,128]{1,0:T(8,128)(2,1)} %param.18) | copy-start | bytes 393220
  7.2 92.2 %all-gather.4.cloned.1.call-start = ((), (), s32[]{:S(2)}) async-start(), calls=%async_computation.7 | async-start | bytes 2129920 | tf_op jit(solution)/shard_map/all_gather | solution.py:56
  19.0 15.3 %copy-start.8 = (bf16[128,512]{1,0:T(8,128)(2,1)}, bf16[128,512]{1,0:T(8,128)(2,1)S(1)}, u32[]{:S(2)}) copy-start(bf16[128,512]{1,0:T(8,128)(2,1)S(1)} %all_gather.16) | copy-start | bytes 393220
  20.8 156.9 %all-gather.6.cloned.1.call-start = ((), (), s32[]{:S(2)}) async-start(), calls=%async_computation.8 | async-start | bytes 2129920 | tf_op jit(solution)/shard_map/all_gather | solution.py:57
  22.6 325.3 %all-reduce.3.cloned.1.call-start = ((), (), s32[]{:S(2)}) async-start(), calls=%async_computation.9 | async-start | bytes 131072 | tf_op jit(solution)/shard_map/pmax | solution.py:97
  34.3 97.2 %copy-start.6 = (bf16[256,512]{1,0:T(8,128)(2,1)}, bf16[256,512]{1,0:T(8,128)(2,1)S(1)}, u32[]{:S(2)}) copy-start(bf16[256,512]{1,0:T(8,128)(2,1)S(1)} %all_gather.15) | copy-start | bytes 786436
  34.7 72.9 %copy-start.22 = (s32[32,2]{0,1:T(2,128)S(1)}, s32[32,2]{0,1:T(2,128)}, u32[]{:S(2)}) copy-start(s32[32,2]{0,1:T(2,128)} %param.24) | copy-start | bytes 772
  107.6 24.0 %copy-start.13 = (bf16[512,128]{1,0:T(8,128)(2,1)S(1)}, bf16[512,128]{1,0:T(8,128)(2,1)}, u32[]{:S(2)}) copy-start(bf16[512,128]{1,0:T(8,128)(2,1)} %param.19) | copy-start | bytes 393220
  131.5 439.4 %reduce-scatter.19.cloned.1.call-start = ((), (), s32[]{:S(2)}) async-start(), calls=%async_computation.17 | async-start | bytes 4259840
  419.7 3.9 copy-start.1
  430.1 287.0 %reduce-scatter.9.cloned.1.call-start = ((), (), s32[]{:S(2)}) async-start(), calls=%async_computation.10 | async-start | bytes 4259840 | tf_op jit(solution)/shard_map/reduce_scatter | solution.py:144
  440.0 360.6 %all-gather.8.cloned.1.call-start = ((), (), s32[]{:S(2)}) async-start(), calls=%async_computation.11 | async-start | bytes 2129920 | tf_op jit(solution)/shard_map/all_gather | solution.py:159
  721.6 8.5 copy-start.20
  721.7 78.9 %all-to-all-start = ((bf16[64,128,128]{1,2,0:T(8,128)(2,1)}), bf16[64,128,128]{1,2,0:T(8,128)(2,1)S(1)}, u32[]{:S(2)}, u32[]{:S(2)}) async-start(bf16[64,128,128]{1,2,0:T(8,128)(2,1)} %copy_bitcast_fusion.3), calls=%async_computation.1 | async-start | bytes 4194304 | tf_op jit(solution)/shard_map/all_to_all | solution.py:15
  730.1 374.3 %reduce-scatter.15.cloned.1.call-start = ((), (), s32[]{:S(2)}) async-start(), calls=%async_computation.14 | async-start | bytes 4259840 | tf_op jit(solution)/shard_map/reduce_scatter | solution.py:260
  730.5 72.2 %copy-start.11 = (bf16[2,128,2,64]{1,0,3,2:T(2,128)(2,1)}, bf16[2,128,2,64]{1,0,3,2:T(2,128)(2,1)S(1)}, u32[]{:S(2)}) copy-start(bf16[2,128,2,64]{1,0,3,2:T(2,128)(2,1)S(1)} %copy.106) | copy-start | bytes 196612
  961.9 288.7 %reduce-scatter.13.cloned.1.call-start = ((), (), s32[]{:S(2)}) async-start(), calls=%async_computation.13 | async-start | bytes 4259840 | tf_op jit(solution)/shard_map/reduce_scatter | solution.py:257
  971.9 304.5 %reduce-scatter.11.cloned.1.call-start = ((), (), s32[]{:S(2)}) async-start(), calls=%async_computation.12 | async-start | bytes 655360 | tf_op jit(solution)/shard_map/reduce_scatter | solution.py:267
  972.0 132.4 %copy-start.9 = (bf16[128,512]{1,0:T(8,128)(2,1)S(1)}, bf16[128,512]{1,0:T(8,128)(2,1)}, u32[]{:S(2)}) copy-start(bf16[128,512]{1,0:T(8,128)(2,1)} %copy-done.8) | copy-start | bytes 393220
  973.9 491.8 %all-reduce.5.cloned.1.call-start = ((), (), s32[]{:S(2)}) async-start(), calls=%async_computation.16 | async-start | bytes 2097152 | tf_op jit(solution)/shard_map/psum | solution.py:270
  974.3 278.6 %copy-start.15 = (bf16[512,128]{1,0:T(8,128)(2,1)S(1)}, bf16[512,128]{1,0:T(8,128)(2,1)}, u32[]{:S(2)}) copy-start(bf16[512,128]{1,0:T(8,128)(2,1)} %param.20) | copy-start | bytes 393220
  1105.4 147.7 %copy-start.16 = (bf16[512,128]{1,0:T(8,128)(2,1)S(1)}, bf16[512,128]{1,0:T(8,128)(2,1)}, u32[]{:S(2)}) copy-start(bf16[512,128]{1,0:T(8,128)(2,1)} %param.21) | copy-start | bytes 393220
  1105.4 147.7 %copy-start.21 = (f32[128,128]{0,1:T(8,128)S(1)}, f32[128,128]{0,1:T(8,128)}, u32[]{:S(2)}) copy-start(f32[128,128]{0,1:T(8,128)} %reduce-scatter.15.cloned.1.call-done) | copy-start | bytes 196612
  1252.8 236.1 %reduce-scatter.17.cloned.1.call-start = ((), (), s32[]{:S(2)}) async-start(), calls=%async_computation.15 | async-start | bytes 327680 | tf_op jit(solution)/shard_map/reduce_scatter | solution.py:268
  (28 other events, 49.5 us)
Sparse Core Ops, SparseCore 0:
  20.9 78.4 all-gather.3
  102.7 74.9 all-gather.5
  181.8 166.0 all-reduce.2
  430.2 140.7 reduce-scatter.18
  574.9 142.0 reduce-scatter.8
  720.4 80.1 all-gather.7
  962.1 142.2 reduce-scatter.14
  1108.5 142.0 reduce-scatter.12
  1253.3 23.0 reduce-scatter.10
  1280.6 184.9 all-reduce.4
  1468.2 20.7 reduce-scatter.16
